TPU v7x, 512 devices: a whole 4x8x8 slice. The times are simulated.
512 devices in a mesh: section: 2 (over core), ha: 8 (over z_hi, x), wa: 32 (over z_lo, y).
Axes of the slice: x: 4, y: 8, z: 8 (z_hi: 2, z_lo: 4; z = z_hi * 4 + z_lo), core: 2. Of those that a mesh axis runs over, the one named last changes fastest.
Arguments:
- slide_tiles: bfloat16 [2, 96, 128, 4096], P('section', None, 'ha', 'wa'), may hold values from -6 to 6
- depth_kernel: float32 [3, 96, 7, 7], replicated, may hold values from -0.875 to 0.875
- depth_bias: float32 [3, 96], replicated, may hold values from -3 to 3
- norm_gain: float32 [3, 96], replicated, may hold values from 0.5 to 2
- norm_shift: float32 [3, 96], replicated, may hold values from -3 to 3
- expand_weight: bfloat16 [3, 96, 384], P(None, None, 'section'), may hold values from -0.625 to 0.625
- expand_bias: float32 [3, 384], replicated, may hold values from -3 to 3
- project_weight: bfloat16 [3, 384, 96], P(None, 'section'), may hold values from -0.3125 to 0.3125
- project_bias: float32 [3, 96], replicated, may hold values from -3 to 3
- layer_scale: float32 [3, 96], replicated, may hold values from 0.3 to 1.5
Outputs:
- section_output: bfloat16 [2, 96, 128, 4096], P('section', None, 'ha', 'wa')
All inputs are finite; a program needn't handle non-finite values.
Results may differ from a plain program's by a relative error of at most 0.014.
Values may be sent and summed in bfloat16 or wider, within the bound.
A program may use at most 64 MiB of HBM per device.

v0:
```python
import functools

import jax
import jax.numpy as jnp
from jax import lax
from jax.experimental import pallas as pl
from jax.experimental.pallas import tpu as pltpu
from jax.sharding import PartitionSpec as P

EPSILON = 1e-06
MESH = pl.DeviceIdType.MESH
BF16, F32 = jnp.bfloat16, jnp.float32

AROUND = ((-1, -1), (-1, 0), (-1, 1), (0, -1), (0, 1), (1, -1), (1, 0), (1, 1))
UP, DOWN = 1, 6
REACH = 3
ROWS = 4


def columns_of(row):
    return jnp.broadcast_to(row, (128, row.shape[1])).T


def kernel(
    axis_sizes,
    tile_ref,
    taps_ref,
    dbias_ref,
    gain_ref,
    shift_ref,
    expand_ref,
    ebias_ref,
    project_ref,
    pbias_ref,
    scale_ref,
    out_ref,
    state,
    packed,
    row_halo,
    col_halo,
    shifted,
    taps,
    vectors,
    first,
    second,
    conv,
    normed,
    send_sem,
    recv_sem,
    wsend_sem,
    wrecv_sem,
):
    blocks = packed.shape[0]
    rows, channels = state.shape[1], state.shape[2]
    half = first.shape[2]
    section, ha, wa = (lax.axis_index(a) for a in ("section", "ha", "wa"))
    n_ha, n_wa = axis_sizes
    here = []
    for dy, dx in AROUND:
        inside = jnp.bool_(True)
        if dy:
            inside = jnp.logical_and(inside, ha > 0 if dy < 0 else ha < n_ha - 1)
        if dx:
            inside = jnp.logical_and(inside, wa > 0 if dx < 0 else wa < n_wa - 1)
        here.append(inside)

    def device(d):
        dy, dx = AROUND[d]
        return (section, ha + dy, wa + dx)

    row_halo[...] = jnp.zeros_like(row_halo)
    col_halo[...] = jnp.zeros_like(col_halo)

    barrier = pltpu.get_barrier_semaphore()
    for d in range(8):

        @pl.when(here[d])
        def _(d=d):
            pl.semaphore_signal(barrier, inc=1, device_id=device(d), device_id_type=MESH)

    partner = (1 - section, ha, wa)
    pl.semaphore_signal(barrier, inc=1, device_id=partner, device_id_type=MESH)

    for b in range(blocks):
        bias = jnp.where(section == 0, ebias_ref[b : b + 1, :half], ebias_ref[b : b + 1, half:])
        parts = []
        for _ in range(3):
            part = bias.astype(BF16).astype(F32)
            bias = bias - part
            parts.append(part)
        whole = jnp.concatenate(
            [expand_ref[b].astype(F32)] + parts + [jnp.zeros((128 - channels - 3, half), F32)], axis=0
        )
        first[0, b] = whole.T.astype(BF16)
        second[0, b] = project_ref[b].astype(F32).T.astype(BF16)
        scale = scale_ref[b : b + 1, :]
        for k, row in enumerate(
            (dbias_ref[b : b + 1, :], gain_ref[b : b + 1, :], shift_ref[b : b + 1, :], scale, scale * pbias_ref[b : b + 1, :])
        ):
            vectors[b, k] = columns_of(row)

    def spread(i, carry):
        for b in range(blocks):
            for j in range(7):
                taps[b, i * 7 + j] = columns_of(taps_ref[b, i, j : j + 1, :])
        return carry

    lax.fori_loop(0, 7, spread, 0)
    ones = lax.broadcasted_iota(jnp.int32, (128 - channels, ROWS * 128), 0) < 3
    normed[channels:, :] = jnp.where(ones, 1.0, 0.0).astype(BF16)
    state[0] = jnp.swapaxes(tile_ref[...], 0, 1)

    lane = lax.broadcasted_iota(jnp.int32, (channels, 128), 1)

    def pack(b):
        kept = jnp.zeros((channels, 128), BF16)
        for h in range(rows):
            kept = jnp.where(lane // 8 == h, pltpu.roll(state[b, h], 8 * h + REACH, 1), kept)
        packed[b] = kept

    pack(0)
    greeted = jnp.int32(1)
    for d in range(8):
        greeted = greeted + here[d].astype(jnp.int32)
    pl.semaphore_wait(barrier, greeted)

    weights = [
        pltpu.make_async_remote_copy(
            src_ref=ref.at[0], dst_ref=ref.at[1], send_sem=wsend_sem.at[k], recv_sem=wrecv_sem.at[k],
            device_id=partner, device_id_type=MESH,
        )
        for k, ref in enumerate((first, second))
    ]

    def copy(b, d):
        if d == UP:
            source, target = state.at[b, pl.ds(0, REACH)], row_halo.at[b, 1]
        elif d == DOWN:
            source, target = state.at[b, pl.ds(rows - REACH, REACH)], row_halo.at[b, 0]
        else:
            source, target = packed.at[b], col_halo.at[b, 7 - d]
        return pltpu.make_async_remote_copy(
            src_ref=source, dst_ref=target, send_sem=send_sem.at[b, d], recv_sem=recv_sem.at[b, 7 - d],
            device_id=device(d), device_id_type=MESH,
        )

    def send(b):
        for d in (3, 4, UP, DOWN, 0, 2, 5, 7):

            @pl.when(here[d])
            def _(d=d):
                copy(b, d).start()

    def receive(b, which):
        for d in which:

            @pl.when(here[d])
            def _(d=d):
                copy(b, 7 - d).wait_recv()

    def lay_out(b, at, row, ends):
        for j in range(7):
            s = REACH - j
            if s > 0:
                moved = pltpu.roll(jnp.where(lane >= 128 - s, ends, row), s, 1)
            elif s < 0:
                moved = pltpu.roll(jnp.where(lane < -s, ends, row), 128 + s, 1)
            else:
                moved = row
            shifted[j, at] = moved.astype(F32)

    def ends_of(b, left, right, h):
        both = jnp.where(lane % 8 < REACH, col_halo[b, left], col_halo[b, right])
        return pltpu.roll(both, 128 - (8 * h + REACH), 1)

    def chunk(b, at):
        def group(g, carry):
            part = pl.ds(pl.multiple_of(g * 8, 8), 8)
            total = jnp.broadcast_to(vectors[b, 0, part, :][None], (ROWS, 8, 128))
            for j in range(7):
                source = shifted[j, pl.ds(at, ROWS + 6), part, :]
                for i in range(7):
                    total = total + source[i : i + ROWS] * taps[b, i * 7 + j, part, :][None]
            conv[:, part, :] = total
            return carry

        lax.fori_loop(0, channels // 8, group, 0)
        for k in range(ROWS):
            value = conv[k]
            centred = value - jnp.mean(value, axis=0, keepdims=True)
            variance = jnp.mean(centred * centred, axis=0, keepdims=True)
            normed[:channels, k * 128 : (k + 1) * 128] = (
                centred * lax.rsqrt(variance + EPSILON) * vectors[b, 1] + vectors[b, 2]
            ).astype(BF16)
        projected = None
        for s in range(2):
            hidden = jnp.dot(first[s, b], normed[...], preferred_element_type=F32)
            activated = (0.5 * hidden * (1.0 + lax.erf(hidden * (2.0**-0.5)))).astype(BF16)
            part = jnp.dot(second[s, b], activated, preferred_element_type=F32)
            projected = part if projected is None else projected + part
        for k in range(ROWS):
            value = (
                state[b, at + k].astype(F32)
                + vectors[b, 3] * projected[:, k * 128 : (k + 1) * 128]
                + vectors[b, 4]
            ).astype(BF16)
            state[b + 1, at + k] = value

    send(0)
    for copy_of in weights:
        copy_of.start()
    for b in range(blocks):
        receive(b, (3, 4))
        for h in range(rows):
            lay_out(b, REACH + h, state[b, h], ends_of(b, 3, 4, h))
        if b == 0:
            for copy_of in weights:
                copy_of.wait_recv()

        def middle(c, carry, b=b):
            chunk(b, c * ROWS)
            return carry

        lax.fori_loop(1, rows // ROWS - 1, middle, 0)
        receive(b, (0, 1, 2, 5, 6, 7))
        for k in range(REACH):
            lay_out(b, k, row_halo[b, 0, k], ends_of(b, 0, 2, rows - REACH + k))
            lay_out(b, rows + REACH + k, row_halo[b, 1, k], ends_of(b, 5, 7, k))

        def outer(c, carry, b=b):
            chunk(b, c * (rows - ROWS))
            return carry

        lax.fori_loop(0, 2, outer, 0)
        if b + 1 < blocks:
            pack(b + 1)
            send(b + 1)
    out_ref[...] = jnp.swapaxes(state[blocks], 0, 1)

    for copy_of in weights:
        copy_of.wait_send()
    for b in range(blocks):
        for d in range(8):

            @pl.when(here[d])
            def _(b=b, d=d):
                copy(b, d).wait_send()


def solution(mesh):
    n_ha, n_wa = mesh.shape["ha"], mesh.shape["wa"]

    def body(tiles, taps, dbias, gain, shift, expand, ebias, project, pbias, scale):
        blocks, channels = dbias.shape
        rows, width = tiles.shape[2:]
        half = expand.shape[2]
        vmem = pl.BlockSpec(memory_space=pltpu.VMEM)
        result = pl.pallas_call(
            functools.partial(kernel, (n_ha, n_wa)),
            out_shape=jax.ShapeDtypeStruct((channels, rows, width), BF16),
            in_specs=[vmem] * 10,
            out_specs=vmem,
            scratch_shapes=[
                pltpu.VMEM((blocks + 1, rows, channels, width), BF16),
                pltpu.VMEM((blocks, channels, width), BF16),
                pltpu.VMEM((blocks, 2, REACH, channels, width), BF16),
                pltpu.VMEM((blocks, 8, channels, width), BF16),
                pltpu.VMEM((7, rows + 2 * REACH, channels, width), F32),
                pltpu.VMEM((blocks, 49, channels, 128), F32),
                pltpu.VMEM((blocks, 5, channels, 128), F32),
                pltpu.VMEM((2, blocks, half, 128), BF16),
                pltpu.VMEM((2, blocks, channels, half), BF16),
                pltpu.VMEM((ROWS, channels, width), F32),
                pltpu.VMEM((128, ROWS * width), BF16),
                pltpu.SemaphoreType.DMA((blocks, 8)),
                pltpu.SemaphoreType.DMA((blocks, 8)),
                pltpu.SemaphoreType.DMA((2,)),
                pltpu.SemaphoreType.DMA((2,)),
            ],
            compiler_params=pltpu.CompilerParams(
                collective_id=0, has_side_effects=True, vmem_limit_bytes=52 * 2**20
            ),
        )(tiles[0], jnp.transpose(taps, (0, 2, 3, 1)), dbias, gain, shift, expand, ebias, project, pbias, scale)
        return result[None]

    return jax.shard_map(
        body,
        mesh=mesh,
        in_specs=(
            P("section", None, "ha", "wa"),
            P(),
            P(),
            P(),
            P(),
            P(None, None, "section"),
            P(),
            P(None, "section", None),
            P(),
            P(),
        ),
        out_specs=P("section", None, "ha", "wa"),
        check_vma=False,
    )
```

profile of v0, /device:TPU:70, one launch (start us, length us, event | category | flops | bytes accessed | tf_op | source)
XLA Modules:
  0.0 61.5 jit_solution(7271994221261166089)
XLA Ops:
  0.0 0.0 copy-start.5
  0.0 0.7 %copy-done.5 = f32[3,96]{1,0:T(4,128)S(1)} copy-done((f32[3,96]{1,0:T(4,128)S(1)}, f32[3,96]{1,0:T(4,128)}, u32[]{:S(2)}) %copy-start.5) | copy-done | bytes 1176
  0.7 0.0 copy-start
  0.7 1.0 %copy-done = bf16[1,96,16,128]{3,2,1,0:T(8,128)(2,1)S(1)} copy-done((bf16[1,96,16,128]{3,2,1,0:T(8,128)(2,1)S(1)}, bf16[1,96,16,128]{3,2,1,0:T(8,128)(2,1)}, u32[]{:S(2)}) %copy-start) | copy-done | bytes 393240
  1.7 0.0 copy-start.1
  1.7 0.9 %copy-done.1 = bf16[3,96,192]{2,1,0:T(8,128)(2,1)S(1)} copy-done((bf16[3,96,192]{2,1,0:T(8,128)(2,1)S(1)}, bf16[3,96,192]{2,1,0:T(8,128)(2,1)}, u32[]{:S(2)}) %copy-start.1) | copy-done | bytes 110616
  2.6 0.0 copy-start.2
  2.6 0.9 %copy-done.2 = bf16[3,192,96]{2,1,0:T(8,128)(2,1)S(1)} copy-done((bf16[3,192,96]{2,1,0:T(8,128)(2,1)S(1)}, bf16[3,192,96]{2,1,0:T(8,128)(2,1)}, u32[]{:S(2)}) %copy-start.2) | copy-done | bytes 110616
  3.5 0.0 copy-start.3
  3.5 0.9 %copy-done.3 = f32[3,96,7,7]{1,3,2,0:T(8,128)S(1)} copy-done((f32[3,96,7,7]{1,3,2,0:T(8,128)S(1)}, f32[3,96,7,7]{1,3,2,0:T(8,128)}, u32[]{:S(2)}) %copy-start.3) | copy-done | bytes 56472
  4.4 0.0 copy-start.4
  4.4 0.7 %copy-done.4 = f32[3,384]{1,0:T(4,128)S(1)} copy-done((f32[3,384]{1,0:T(4,128)S(1)}, f32[3,384]{1,0:T(4,128)}, u32[]{:S(2)}) %copy-start.4) | copy-done | bytes 4632
  5.1 0.0 copy-start.6
  5.1 0.7 %copy-done.6 = f32[3,96]{1,0:T(4,128)S(1)} copy-done((f32[3,96]{1,0:T(4,128)S(1)}, f32[3,96]{1,0:T(4,128)}, u32[]{:S(2)}) %copy-start.6) | copy-done | bytes 1176
  5.8 0.0 copy-start.7
  5.8 0.7 %copy-done.7 = f32[3,96]{1,0:T(4,128)S(1)} copy-done((f32[3,96]{1,0:T(4,128)S(1)}, f32[3,96]{1,0:T(4,128)}, u32[]{:S(2)}) %copy-start.7) | copy-done | bytes 1176
  6.4 0.0 copy-start.8
  6.4 0.7 %copy-done.8 = f32[3,96]{1,0:T(4,128)S(1)} copy-done((f32[3,96]{1,0:T(4,128)S(1)}, f32[3,96]{1,0:T(4,128)}, u32[]{:S(2)}) %copy-start.8) | copy-done | bytes 1176
  7.1 0.0 copy-start.9
  7.1 0.7 %copy-done.9 = f32[3,96]{1,0:T(4,128)S(1)} copy-done((f32[3,96]{1,0:T(4,128)S(1)}, f32[3,96]{1,0:T(4,128)}, u32[]{:S(2)}) %copy-start.9) | copy-done | bytes 1176
  7.8 52.9 %shard_map.100 = bf16[96,16,128]{2,1,0:T(8,128)(2,1)S(1)} custom-call(bf16[96,16,128]{2,1,0:T(8,128)(2,1)S(1)} %bitcast.4, f32[3,7,7,96]{3,2,1,0:T(8,128)S(1)} %bitcast.5, f32[3,96]{1,0:T(4,128)S(1)} %copy-done.5, f32[3,96]{1,0:T(4,128)S(1)} %copy-done.6, f32[3,96]{1,0:T(4,128)S(1)} %copy-done.7, bf16[3,96,192]{2,1,0:T(8,128)(2,1)S(1)} %copy-done.1, ...), custom_call_target="tpu_custom_call" | custom-call | tf_op jit(solution)/shard_map/pallas_call | solution.py:258
  60.8 0.7 %copy.12 = bf16[1,96,16,128]{3,2,1,0:T(8,128)(2,1)} copy(bf16[1,96,16,128]{3,2,1,0:T(8,128)(2,1)S(1)} %bitcast.3) | data formatting | bytes 786432
Async XLA Ops:
  0.0 0.7 %copy-start.5 = (f32[3,96]{1,0:T(4,128)S(1)}, f32[3,96]{1,0:T(4,128)}, u32[]{:S(2)}) copy-start(f32[3,96]{1,0:T(4,128)} %dbias_ref.1) | copy-start | bytes 3460
  0.7 1.0 %copy-start = (bf16[1,96,16,128]{3,2,1,0:T(8,128)(2,1)S(1)}, bf16[1,96,16,128]{3,2,1,0:T(8,128)(2,1)}, u32[]{:S(2)}) copy-start(bf16[1,96,16,128]{3,2,1,0:T(8,128)(2,1)} %param.10) | copy-start | bytes 1179652
  1.7 0.9 %copy-start.1 = (bf16[3,96,192]{2,1,0:T(8,128)(2,1)S(1)}, bf16[3,96,192]{2,1,0:T(8,128)(2,1)}, u32[]{:S(2)}) copy-start(bf16[3,96,192]{2,1,0:T(8,128)(2,1)} %expand_ref.1) | copy-start | bytes 331780
  2.6 0.9 %copy-start.2 = (bf16[3,192,96]{2,1,0:T(8,128)(2,1)S(1)}, bf16[3,192,96]{2,1,0:T(8,128)(2,1)}, u32[]{:S(2)}) copy-start(bf16[3,192,96]{2,1,0:T(8,128)(2,1)} %project_ref.1) | copy-start | bytes 331780
  3.5 0.9 %copy-start.3 = (f32[3,96,7,7]{1,3,2,0:T(8,128)S(1)}, f32[3,96,7,7]{1,3,2,0:T(8,128)}, u32[]{:S(2)}) copy-start(f32[3,96,7,7]{1,3,2,0:T(8,128)} %param.11) | copy-start | bytes 169348
  4.4 0.7 %copy-start.4 = (f32[3,384]{1,0:T(4,128)S(1)}, f32[3,384]{1,0:T(4,128)}, u32[]{:S(2)}) copy-start(f32[3,384]{1,0:T(4,128)} %ebias_ref.1) | copy-start | bytes 13828
  5.1 0.7 %copy-start.6 = (f32[3,96]{1,0:T(4,128)S(1)}, f32[3,96]{1,0:T(4,128)}, u32[]{:S(2)}) copy-start(f32[3,96]{1,0:T(4,128)} %gain_ref.1) | copy-start | bytes 3460
  5.8 0.7 %copy-start.7 = (f32[3,96]{1,0:T(4,128)S(1)}, f32[3,96]{1,0:T(4,128)}, u32[]{:S(2)}) copy-start(f32[3,96]{1,0:T(4,128)} %shift_ref.1) | copy-start | bytes 3460
  6.4 0.7 %copy-start.8 = (f32[3,96]{1,0:T(4,128)S(1)}, f32[3,96]{1,0:T(4,128)}, u32[]{:S(2)}) copy-start(f32[3,96]{1,0:T(4,128)} %pbias_ref.1) | copy-start | bytes 3460
  7.1 0.7 %copy-start.9 = (f32[3,96]{1,0:T(4,128)S(1)}, f32[3,96]{1,0:T(4,128)}, u32[]{:S(2)}) copy-start(f32[3,96]{1,0:T(4,128)} %scale_ref.1) | copy-start | bytes 3460
where the time goes:
time: 61.9 us; the launch traced here: 61.5 us
  Pallas kernels  52.9 us (85%)
  local copies, waits for them, and re-layouts  8.55 us (14%)
    pallas_call x1, Pallas kernels, body(): pl.pallas_call(functools.partial(kernel, (n_ha, n_wa)), out_shape=jax.Sha...  52.9 us
    unnamed x21, local copies, waits for them, and re-layouts  8.55 us

commit v1 on v0

v1 whole, which is shorter than its diff:
```python
import functools

import jax
import jax.numpy as jnp
from jax import lax
from jax.experimental import pallas as pl
from jax.experimental.pallas import tpu as pltpu
from jax.sharding import PartitionSpec as P

EPSILON = 1e-06
MESH = pl.DeviceIdType.MESH
BF16, F32 = jnp.bfloat16, jnp.float32

AROUND = ((-1, -1), (-1, 0), (-1, 1), (0, -1), (0, 1), (1, -1), (1, 0), (1, 1))
UP, LEFT, RIGHT, DOWN = 1, 3, 4, 6
REACH = 3
ROWS = 4
DEPTH_BIAS, GAIN, SHIFT, SCALE, OFFSET = range(49, 54)
PIECE = 128


def columns_of(row):
    return jnp.broadcast_to(row, (128, row.shape[1])).T


def gelu(hidden):
    return (0.5 * hidden * (1.0 + lax.erf(hidden * (2.0**-0.5)))).astype(BF16)


def kernel(
    axis_sizes,
    tile_hbm,
    taps_hbm,
    dbias_hbm,
    gain_hbm,
    shift_hbm,
    expand_hbm,
    ebias_hbm,
    project_hbm,
    pbias_hbm,
    scale_hbm,
    out_ref,
    tile_ref,
    taps_ref,
    dbias_ref,
    gain_ref,
    shift_ref,
    expand_ref,
    ebias_ref,
    project_ref,
    pbias_ref,
    scale_ref,
    state,
    packed,
    row_halo,
    col_halo,
    ends,
    shifted,
    values,
    compact,
    wide,
    first,
    halves,
    second,
    conv,
    normed,
    active,
    projected,
    load_sem,
    send_sem,
    recv_sem,
    wsend_sem,
    wrecv_sem,
):
    blocks, rows, channels = packed.shape[0], state.shape[1], state.shape[2]
    half = halves.shape[3]
    groups, pieces = channels // 8, 2 * half // PIECE
    section, ha, wa = (lax.axis_index(a) for a in ("section", "ha", "wa"))
    n_ha, n_wa = axis_sizes
    here = []
    for dy, dx in AROUND:
        inside = jnp.bool_(True)
        if dy:
            inside = jnp.logical_and(inside, ha > 0 if dy < 0 else ha < n_ha - 1)
        if dx:
            inside = jnp.logical_and(inside, wa > 0 if dx < 0 else wa < n_wa - 1)
        here.append(inside)
    low_first = ha < n_ha // 2

    def device(d):
        dy, dx = AROUND[d]
        return (section, ha + dy, wa + dx)

    for d in range(8):

        @pl.when(jnp.logical_not(here[d]))
        def _(d=d):
            def clear(b, carry):
                if d in (UP, DOWN):
                    row_halo[b, int(d == DOWN)] = jnp.zeros(row_halo.shape[2:], BF16)
                else:
                    col_halo[b, d] = jnp.zeros(col_halo.shape[2:], BF16)
                if d in (LEFT, RIGHT):
                    col_halo[b, 5 + d] = jnp.zeros(col_halo.shape[2:], BF16)
                return carry

            lax.fori_loop(0, blocks, clear, 0)

    barrier = pltpu.get_barrier_semaphore()
    for d in range(8):

        @pl.when(here[d])
        def _(d=d):
            pl.semaphore_signal(barrier, inc=1, device_id=device(d), device_id_type=MESH)

    partner = (1 - section, ha, wa)
    pl.semaphore_signal(barrier, inc=1, device_id=partner, device_id_type=MESH)

    loads = [
        pltpu.make_async_copy(source, target, load_sem.at[k])
        for k, (source, target) in enumerate(
            (
                (tile_hbm, tile_ref),
                (expand_hbm, expand_ref),
                (ebias_hbm, ebias_ref),
                (project_hbm, project_ref),
                (taps_hbm, taps_ref),
                (dbias_hbm, dbias_ref),
                (gain_hbm, gain_ref),
                (shift_hbm, shift_ref),
                (pbias_hbm, pbias_ref),
                (scale_hbm, scale_ref),
            )
        )
    ]
    for load in loads:
        load.start()

    lane = lax.broadcasted_iota(jnp.int32, (channels, 128), 1)
    lane_group = lane // 8
    from_left = lane % 8 < REACH

    def pack(b, part):
        kept = jnp.zeros((channels, 128), BF16)
        for h in range(rows):
            kept = jnp.where(lane_group == h, pltpu.roll(state[b, h], (8 * h + REACH) % 128, 1), kept)
        packed[b, part] = kept

    def copy(b, d, part):
        place, landing = d, 7 - d
        if d == UP:
            source, target = state.at[b, pl.ds(0, REACH)], row_halo.at[b, 1]
        elif d == DOWN:
            source, target = state.at[b, pl.ds(rows - REACH, REACH)], row_halo.at[b, 0]
        else:
            if d in (LEFT, RIGHT):
                place, landing = d + 5 * part, 7 - d + 5 * part
            source, target = packed.at[b, part], col_halo.at[b, landing]
        return pltpu.make_async_remote_copy(
            src_ref=source,
            dst_ref=target,
            send_sem=send_sem.at[b, place],
            recv_sem=recv_sem.at[b, landing],
            device_id=device(d),
            device_id_type=MESH,
        )

    def start(c):
        c.start()

    def wait_send(c):
        c.wait_send()

    def each(b, which, act, part=0, condition=None):
        for d in which:

            @pl.when(here[d] if condition is None else jnp.logical_and(here[d], condition))
            def _(d=d):
                act(copy(b, d, part))

    def receive(b, which, part=0, condition=None):
        for d in which:

            @pl.when(here[d] if condition is None else jnp.logical_and(here[d], condition))
            def _(d=d):
                copy(b, 7 - d, part).wait_recv()

    loads[0].wait()
    state[0] = jnp.swapaxes(tile_ref[...], 0, 1)
    pack(0, 0)
    for load in loads[1:4]:
        load.wait()

    def prepare(b, carry):
        one = pl.ds(b, 1)
        bias = jnp.where(section == 0, ebias_ref[one, :half], ebias_ref[one, half:])
        parts = []
        for _ in range(3):
            part = bias.astype(BF16).astype(F32)
            bias = bias - part
            parts.append(part)
        whole = jnp.concatenate(
            [expand_ref[b].astype(F32)] + parts + [jnp.zeros((128 - channels - 3, half), F32)], axis=0
        )
        first[b, :half, :] = whole.T.astype(BF16)
        halves[0, b] = project_ref[b].astype(F32).T.astype(BF16)
        return carry

    lax.fori_loop(0, blocks, prepare, 0)

    greeted = jnp.int32(1)
    for d in range(8):
        greeted = greeted + here[d].astype(jnp.int32)
    pl.semaphore_wait(barrier, greeted)

    each(0, (LEFT, RIGHT, UP, DOWN, 0, 2, 5, 7), start)
    weights = [
        pltpu.make_async_remote_copy(
            src_ref=source,
            dst_ref=target,
            send_sem=wsend_sem.at[k],
            recv_sem=wrecv_sem.at[k],
            device_id=partner,
            device_id_type=MESH,
        )
        for k, (source, target) in enumerate(
            ((first.at[:, pl.ds(0, half)], first.at[:, pl.ds(half, half)]), (halves.at[0], halves.at[1]))
        )
    ]
    for c in weights:
        c.start()

    ones = lax.broadcasted_iota(jnp.int32, (128 - channels, ROWS * 128), 0) < 3
    normed[channels:, :] = jnp.where(ones, 1.0, 0.0).astype(BF16)
    normed[:channels, :] = jnp.zeros((channels, ROWS * 128), BF16)
    active[...] = jnp.zeros_like(active)
    projected[...] = jnp.zeros_like(projected)
    for load in loads[4:]:
        load.wait()

    values[...] = jnp.zeros_like(values)

    def gather(b, carry):
        one = pl.ds(b, 1)
        scale = scale_ref[one, :]
        places = [(7 * i, 7, taps_ref[b, i]) for i in range(7)]
        for k, row in enumerate(
            (dbias_ref[one, :], gain_ref[one, :], shift_ref[one, :], scale, scale * pbias_ref[one, :])
        ):
            places.append((49 + k, 1, row))
        for place, size, row in places:
            main = row.astype(BF16).astype(F32)
            values[pl.ds(place, size), :] = main
            values[pl.ds(64 + place, size), :] = row - main
        compact[b] = values[...].T.astype(BF16)
        return carry

    lax.fori_loop(0, blocks, gather, 0)
    n_values = wide.shape[0]
    every = jnp.full((128, 128), 1.0, BF16)

    def spread(b, n, count):
        kept = [jnp.where(lane % 64 == n + k, compact[b], jnp.zeros((channels, 128), BF16)) for k in range(count)]
        over = jnp.dot(jnp.concatenate(kept, axis=0), every, preferred_element_type=F32)
        wide[pl.ds(n, count)] = over.reshape(count, channels, 128)

    def lay_out(at, row):
        beyond = ends[at]
        for j in range(7):
            s = REACH - j
            if s > 0:
                moved = pltpu.roll(jnp.where(lane >= 128 - s, beyond, row), s, 1)
            elif s < 0:
                moved = pltpu.roll(jnp.where(lane < -s, beyond, row), 128 + s, 1)
            else:
                moved = row
            shifted[j, at] = moved.astype(F32)

    def lay_out_own(b, begin, chunks):
        def some(c, carry):
            for k in range(ROWS):
                h = begin + c * ROWS + k
                lay_out(REACH + h, state[b, h])
            return carry

        lax.fori_loop(0, chunks, some, 0)

    def lay_out_halo(b, side):
        both = jnp.where(from_left, col_halo[b, 5 * side], col_halo[b, 5 * side + 2])
        for k in range(REACH):
            at = side * (rows + REACH) + k
            h = jnp.where(side == 1, k, rows - REACH + k)
            ends[at] = pltpu.roll(both, 128 - REACH - 8 * h, 1)
            lay_out(at, row_halo[b, side, k])

    def conv_group(at, g):
        part = pl.ds(pl.multiple_of(g * 8, 8), 8)
        total = jnp.broadcast_to(wide[DEPTH_BIAS, part, :][None], (ROWS, 8, 128))
        for j in range(7):
            source = shifted[j, pl.ds(at, ROWS + 6), part, :]
            for i in range(7):
                total = total + source[i : i + ROWS] * wide[i * 7 + j, part, :][None]
        conv[:, part, :] = total

    def normalise():
        for k in range(ROWS):
            value = conv[k]
            centred = value - jnp.mean(value, axis=0, keepdims=True)
            variance = jnp.mean(centred * centred, axis=0, keepdims=True)
            normed[:channels, k * 128 : (k + 1) * 128] = (
                centred * lax.rsqrt(variance + EPSILON) * wide[GAIN] + wide[SHIFT]
            ).astype(BF16)

    def finish(b, at, update):
        for k in range(ROWS):
            state[b + 1, at + k] = (
                state[b, at + k].astype(F32) + wide[SCALE] * update[:, k * 128 : (k + 1) * 128] + wide[OFFSET]
            ).astype(BF16)

    def pointwise(b, at):
        hidden = jnp.dot(first[b], normed[...], preferred_element_type=F32)
        finish(b, at, jnp.dot(second[b], gelu(hidden), preferred_element_type=F32))

    def convolve_beside(b, at, before, meant):
        def piece_of(p):
            return pl.ds(pl.multiple_of(p * PIECE, PIECE), PIECE)

        def some(p, carry):
            last = piece_of(jnp.maximum(p - 1, 0))
            update = jnp.dot(second[b, :, last], active[last, :], preferred_element_type=F32)
            projected[...] = jnp.where(p > 0, projected[...] + update, 0.0)
            hidden = jnp.dot(first[b, piece_of(p), :], normed[...], preferred_element_type=F32)
            for k in range(groups // pieces):
                conv_group(at, p * (groups // pieces) + k)
            active[piece_of(p), :] = gelu(hidden)
            return carry

        lax.fori_loop(0, pieces, some, 0)

        @pl.when(meant)
        def _():
            last = piece_of(pieces - 1)
            update = jnp.dot(second[b, :, last], active[last, :], preferred_element_type=F32)
            finish(b, before, projected[...] + update)

        normalise()

    near = jnp.where(low_first, rows - ROWS, 0)
    far = rows - ROWS - near
    inner = jnp.where(low_first, rows - 2 * ROWS, ROWS)
    other = rows - ROWS - inner

    def hand_on(b, which):
        is_low = low_first == (which == 0)
        pack(b, which)
        each(b, (LEFT, RIGHT), start, which)
        each(b, (DOWN, 5, 7), start, which, is_low)
        each(b, (UP, 0, 2), start, which, jnp.logical_not(is_low))

    def block(b, carry):
        def spread_some(n, c):
            spread(b, n * 6, 6)
            return c

        lax.fori_loop(0, n_values // 6, spread_some, 0)

        @pl.when(b == 0)
        def _():
            for c in weights:
                c.wait_recv()

            def join(n, c):
                second[n] = jnp.concatenate([halves[0, n], halves[1, n]], axis=1)
                return c

            lax.fori_loop(0, blocks, join, 0)

        def chunk(k, carry):
            at = jnp.where(k == 0, inner, jnp.where(k == 1, other, jnp.where(k == 2, near, far)))
            before = jnp.where(k == 1, inner, other)
            which = k - 2

            @pl.when(jnp.logical_or(k == 0, jnp.logical_and(k == 1, b > 0)))
            def _():
                receive(b, (LEFT, RIGHT), k)
                both = jnp.where(from_left, col_halo[b, LEFT + 5 * k], col_halo[b, RIGHT + 5 * k])
                for h in range(rows):
                    ends[REACH + h] = pltpu.roll(both, 128 - (8 * h + REACH), 1)
                begin = jnp.where(k == 1, far, jnp.where(jnp.logical_and(low_first, b > 0), ROWS, 0))
                lay_out_own(b, begin, jnp.where(k == 1, 1, jnp.where(b > 0, rows // ROWS - 1, rows // ROWS)))

            @pl.when(k >= 2)
            def _():
                is_low = low_first == (which == 0)
                receive(b, (5, 6, 7), condition=is_low)
                receive(b, (0, 1, 2), condition=jnp.logical_not(is_low))
                lay_out_halo(b, jnp.where(is_low, 1, 0))

            convolve_beside(b, at, before, jnp.logical_or(k == 1, k == 2))

            @pl.when(k >= 2)
            def _():
                pointwise(b, at)

                @pl.when(b + 1 < blocks)
                def _():
                    hand_on(b + 1, which)

            return carry

        lax.fori_loop(0, 4, chunk, 0)
        return carry

    lax.fori_loop(0, blocks, block, 0)
    out_ref[...] = jnp.swapaxes(state[blocks], 0, 1)

    for c in weights:
        c.wait_send()

    def drain(b, carry):
        each(b, range(8), wait_send)
        each(b, (LEFT, RIGHT), wait_send, 1, b > 0)
        return carry

    lax.fori_loop(0, blocks, drain, 0)


def solution(mesh):
    n_ha, n_wa = mesh.shape["ha"], mesh.shape["wa"]

    def body(*arrays):
        tiles, taps, dbias, gain, shift, expand, ebias, project, pbias, scale = arrays
        blocks, channels = dbias.shape
        rows, width = tiles.shape[2:]
        half = expand.shape[2]
        operands = (tiles[0], jnp.transpose(taps, (0, 2, 3, 1)), dbias, gain, shift, expand, ebias, project, pbias, scale)
        result = pl.pallas_call(
            functools.partial(kernel, (n_ha, n_wa)),
            out_shape=jax.ShapeDtypeStruct((channels, rows, width), BF16),
            in_specs=[pl.BlockSpec(memory_space=pl.ANY)] * len(operands),
            out_specs=pl.BlockSpec(memory_space=pltpu.VMEM),
            scratch_shapes=[pltpu.VMEM(o.shape, o.dtype) for o in operands]
            + [
                pltpu.VMEM((blocks + 1, rows, channels, width), BF16),
                pltpu.VMEM((blocks, 2, channels, width), BF16),
                pltpu.VMEM((blocks, 2, REACH, channels, width), BF16),
                pltpu.VMEM((blocks, 10, channels, width), BF16),
                pltpu.VMEM((rows + 2 * REACH, channels, width), BF16),
                pltpu.VMEM((7, rows + 2 * REACH, channels, width), F32),
                pltpu.VMEM((128, channels), F32),
                pltpu.VMEM((blocks, channels, 128), BF16),
                pltpu.VMEM((54, channels, 128), F32),
                pltpu.VMEM((blocks, 2 * half, 128), BF16),
                pltpu.VMEM((2, blocks, channels, half), BF16),
                pltpu.VMEM((blocks, channels, 2 * half), BF16),
                pltpu.VMEM((ROWS, channels, width), F32),
                pltpu.VMEM((128, ROWS * width), BF16),
                pltpu.VMEM((2 * half, ROWS * width), BF16),
                pltpu.VMEM((channels, ROWS * width), F32),
                pltpu.SemaphoreType.DMA((len(operands),)),
                pltpu.SemaphoreType.DMA((blocks, 10)),
                pltpu.SemaphoreType.DMA((blocks, 10)),
                pltpu.SemaphoreType.DMA((2,)),
                pltpu.SemaphoreType.DMA((2,)),
            ],
            compiler_params=pltpu.CompilerParams(
                collective_id=0, has_side_effects=True, vmem_limit_bytes=60 * 2**20
            ),
        )(*operands)
        return result[None]

    return jax.shard_map(
        body,
        mesh=mesh,
        in_specs=(
            P("section", None, "ha", "wa"),
            P(),
            P(),
            P(),
            P(),
            P(None, None, "section"),
            P(),
            P(None, "section", None),
            P(),
            P(),
        ),
        out_specs=P("section", None, "ha", "wa"),
        check_vma=False,
    )
```

time: 61.9 us -> 50.1 us (0.81)
  local copies, waits for them, and re-layouts: 8.55 us -> 1.77 us
  Pallas kernels: 52.9 us -> 48.2 us
    unnamed x21 -> x1, local copies, waits for them, and re-layouts: 8.55 us -> 1.77 us
    pallas_call x1, Pallas kernels: 52.9 us -> 48.2 us  [body(): pl.pallas_call(functools.partial(kernel, (n_ha, n_wa)), out_shape=jax.Sha...]
where the time goes in v1:
time: 50.1 us; the launch traced here: 49.9 us
  Pallas kernels  48.2 us (96%)
  local copies, waits for them, and re-layouts  1.77 us (4%)
    pallas_call x1, Pallas kernels, body(): pl.pallas_call(functools.partial(kernel, (n_ha, n_wa)), out_shape=jax.Sha...  48.2 us
    unnamed x1, local copies, waits for them, and re-layouts  1.77 us

profile of v1, /device:TPU:70, one launch (start us, length us, event | category | flops | bytes accessed | tf_op | source)
XLA Modules:
  0.0 49.9 jit_solution(1648599528032306791)
XLA Ops:
  0.0 48.2 %shard_map.100 = bf16[96,16,128]{2,1,0:T(8,128)(2,1)} custom-call(bf16[96,16,128]{2,1,0:T(8,128)(2,1)} %bitcast.4, f32[3,7,7,96]{3,2,1,0:T(8,128)} %bitcast.5, f32[3,96]{1,0:T(4,128)} %dbias_hbm.1, f32[3,96]{1,0:T(4,128)} %gain_hbm.1, f32[3,96]{1,0:T(4,128)} %shift_hbm.1, bf16[3,96,192]{2,1,0:T(8,128)(2,1)} %expand_hbm.1, f32[3,384]{1,0:T(4,128)} %ebias_hbm.1, ...), custom_call_target="tpu_custom_call" | custom-call | tf_op jit(solution)/shard_map/pallas_call | solution.py:437
  48.2 1.8 %copy.12 = bf16[1,96,16,128]{3,2,1,0:T(8,128)(2,1)} copy(bf16[1,96,16,128]{3,2,1,0:T(8,128)(2,1)} %bitcast.3) | data formatting | bytes 786432

commit v2 on v1

--- a/solution.py
+++ b/solution.py
@@ -188,6 +188,12 @@
     loads[0].wait()
     state[0] = jnp.swapaxes(tile_ref[...], 0, 1)
     pack(0, 0)
+    greeted = jnp.int32(1)
+    for d in range(8):
+        greeted = greeted + here[d].astype(jnp.int32)
+    pl.semaphore_wait(barrier, greeted)
+
+    each(0, (LEFT, RIGHT, 0, 2, 5, 7, UP, DOWN), start)
     for load in loads[1:4]:
         load.wait()
 
@@ -208,12 +214,6 @@
 
     lax.fori_loop(0, blocks, prepare, 0)
 
-    greeted = jnp.int32(1)
-    for d in range(8):
-        greeted = greeted + here[d].astype(jnp.int32)
-    pl.semaphore_wait(barrier, greeted)
-
-    each(0, (LEFT, RIGHT, UP, DOWN, 0, 2, 5, 7), start)
     weights = [
         pltpu.make_async_remote_copy(
             src_ref=source,
@@ -305,8 +305,11 @@
     def normalise():
         for k in range(ROWS):
             value = conv[k]
-            centred = value - jnp.mean(value, axis=0, keepdims=True)
-            variance = jnp.mean(centred * centred, axis=0, keepdims=True)
+            value = value - value[:1]
+            average = jnp.sum(value, axis=0, keepdims=True) * (1.0 / channels)
+            squares = jnp.sum(value * value, axis=0, keepdims=True) * (1.0 / channels)
+            centred = value - average
+            variance = jnp.maximum(squares - average * average, 0.0)
             normed[:channels, k * 128 : (k + 1) * 128] = (
                 centred * lax.rsqrt(variance + EPSILON) * wide[GAIN] + wide[SHIFT]
             ).astype(BF16)
@@ -318,8 +321,11 @@
             ).astype(BF16)
 
     def pointwise(b, at):
-        hidden = jnp.dot(first[b], normed[...], preferred_element_type=F32)
-        finish(b, at, jnp.dot(second[b], gelu(hidden), preferred_element_type=F32))
+        kept = []
+        for k in range(2):
+            hidden = jnp.dot(first[b, k * half : (k + 1) * half], normed[...], preferred_element_type=F32)
+            kept.append(gelu(hidden))
+        finish(b, at, jnp.dot(second[b], jnp.concatenate(kept, axis=0), preferred_element_type=F32))
 
     def convolve_beside(b, at, before, meant):
         def piece_of(p):
@@ -353,16 +359,16 @@
     def hand_on(b, which):
         is_low = low_first == (which == 0)
         pack(b, which)
+        each(b, (5, 7, DOWN), start, which, is_low)
+        each(b, (0, 2, UP), start, which, jnp.logical_not(is_low))
         each(b, (LEFT, RIGHT), start, which)
-        each(b, (DOWN, 5, 7), start, which, is_low)
-        each(b, (UP, 0, 2), start, which, jnp.logical_not(is_low))
 
     def block(b, carry):
         def spread_some(n, c):
-            spread(b, n * 6, 6)
+            spread(b, n * 27, 27)
             return c
 
-        lax.fori_loop(0, n_values // 6, spread_some, 0)
+        lax.fori_loop(0, n_values // 27, spread_some, 0)
 
         @pl.when(b == 0)
         def _():

time: 50.1 us -> 48.5 us (0.968)
  the two profiles are of different devices: /device:TPU:70 before, /device:TPU:134 now
where the time goes in v2:
time: 48.5 us; the launch traced here: 48.3 us
  Pallas kernels  46.5 us (96%)
  local copies, waits for them, and re-layouts  1.77 us (4%)
    pallas_call x1, Pallas kernels, body(): pl.pallas_call(functools.partial(kernel, (n_ha, n_wa)), out_shape=jax.Sha...  46.5 us
    unnamed x1, local copies, waits for them, and re-layouts  1.77 us

profile of v2, /device:TPU:134, one launch (start us, length us, event | category | flops | bytes accessed | tf_op | source)
XLA Modules:
  0.0 48.3 jit_solution(11753770464725219421)
XLA Ops:
  0.0 46.5 %shard_map.100 = bf16[96,16,128]{2,1,0:T(8,128)(2,1)} custom-call(bf16[96,16,128]{2,1,0:T(8,128)(2,1)} %bitcast.4, f32[3,7,7,96]{3,2,1,0:T(8,128)} %bitcast.5, f32[3,96]{1,0:T(4,128)} %dbias_hbm.1, f32[3,96]{1,0:T(4,128)} %gain_hbm.1, f32[3,96]{1,0:T(4,128)} %shift_hbm.1, bf16[3,96,192]{2,1,0:T(8,128)(2,1)} %expand_hbm.1, f32[3,384]{1,0:T(4,128)} %ebias_hbm.1, ...), custom_call_target="tpu_custom_call" | custom-call | tf_op jit(solution)/shard_map/pallas_call | solution.py:443
  46.5 1.8 %copy.12 = bf16[1,96,16,128]{3,2,1,0:T(8,128)(2,1)} copy(bf16[1,96,16,128]{3,2,1,0:T(8,128)(2,1)} %bitcast.3) | data formatting | bytes 786432

commit v3 on v2

--- a/solution.py
+++ b/solution.py
@@ -336,9 +336,12 @@
             update = jnp.dot(second[b, :, last], active[last, :], preferred_element_type=F32)
             projected[...] = jnp.where(p > 0, projected[...] + update, 0.0)
             hidden = jnp.dot(first[b, piece_of(p), :], normed[...], preferred_element_type=F32)
-            for k in range(groups // pieces):
+            early = groups // pieces // 2
+            for k in range(early):
                 conv_group(at, p * (groups // pieces) + k)
             active[piece_of(p), :] = gelu(hidden)
+            for k in range(early, groups // pieces):
+                conv_group(at, p * (groups // pieces) + k)
             return carry
 
         lax.fori_loop(0, pieces, some, 0)
@@ -382,9 +385,9 @@
             lax.fori_loop(0, blocks, join, 0)
 
         def chunk(k, carry):
-            at = jnp.where(k == 0, inner, jnp.where(k == 1, other, jnp.where(k == 2, near, far)))
+            which = jnp.where(b + 1 == blocks, 3 - k, k - 2)
+            at = jnp.where(k == 0, inner, jnp.where(k == 1, other, jnp.where(which == 0, near, far)))
             before = jnp.where(k == 1, inner, other)
-            which = k - 2
 
             @pl.when(jnp.logical_or(k == 0, jnp.logical_and(k == 1, b > 0)))
             def _():

time: 48.5 us -> 48.5 us (level)
  no operation moved by 1% of the time
where the time goes in v3:
time: 48.5 us; the launch traced here: 48.3 us
  Pallas kernels  46.5 us (96%)
  local copies, waits for them, and re-layouts  1.77 us (4%)
    pallas_call x1, Pallas kernels, body(): pl.pallas_call(functools.partial(kernel, (n_ha, n_wa)), out_shape=jax.Sha...  46.5 us
    unnamed x1, local copies, waits for them, and re-layouts  1.77 us

profile of v3, /device:TPU:134, one launch (start us, length us, event | category | flops | bytes accessed | tf_op | source)
XLA Modules:
  0.0 48.3 jit_solution(16196313447830553102)
XLA Ops:
  0.0 46.5 %shard_map.100 = bf16[96,16,128]{2,1,0:T(8,128)(2,1)} custom-call(bf16[96,16,128]{2,1,0:T(8,128)(2,1)} %bitcast.4, f32[3,7,7,96]{3,2,1,0:T(8,128)} %bitcast.5, f32[3,96]{1,0:T(4,128)} %dbias_hbm.1, f32[3,96]{1,0:T(4,128)} %gain_hbm.1, f32[3,96]{1,0:T(4,128)} %shift_hbm.1, bf16[3,96,192]{2,1,0:T(8,128)(2,1)} %expand_hbm.1, f32[3,384]{1,0:T(4,128)} %ebias_hbm.1, ...), custom_call_target="tpu_custom_call" | custom-call | tf_op jit(solution)/shard_map/pallas_call | solution.py:446
  46.5 1.8 %copy.12 = bf16[1,96,16,128]{3,2,1,0:T(8,128)(2,1)} copy(bf16[1,96,16,128]{3,2,1,0:T(8,128)(2,1)} %bitcast.3) | data formatting | bytes 786432
